TPU v7x, 256 devices: a whole 4x4x8 slice. The times are simulated.
256 devices in a mesh: row: 8 (over z), col: 16 (over x, y), vox: 2 (over core).
Axes of the slice: x: 4, y: 4, z: 8, core: 2. Of those that a mesh axis runs over, the one named last changes fastest.
Arguments:
- maps: bfloat16 [16384, 2048], P(('row', 'col'), 'vox'), may hold values from -21 to 21
- probes: bfloat16 [16384, 256], P(('row', 'col')), may hold values from -0.046875 to 0.046875
Outputs:
- gram: float32 [16384, 8, 16, 128], P('row', 'vox', 'col')
- basis: float32 [16384, 256], P(('row', 'col', 'vox'))
- factor: float32 [256, 256], replicated
All inputs are finite; a program needn't handle non-finite values.
Results may differ from a plain program's by a relative error of at most 0.004.
Values may be sent and summed in bfloat16 or wider, within the bound.
No kernel may reach another device: no remote copies, remote signals or barrier semaphores. Data moves between devices by JAX's collectives and lax.ppermute only.
A program may use at most 64 MiB of HBM per device.

v0:
```python
import jax
import jax.numpy as jnp
from jax import lax
from jax.sharding import PartitionSpec as P

VOX = 2048


def block_product(piece, partner):
    return (
        lax.dot_general(
            piece, partner, (((1,), (1,)), ((), ())), preferred_element_type=jnp.float32
        )
        / VOX
    )


def shards(maps, probes):
    sub_rows = maps.shape[0]
    row_count = lax.axis_size("row")
    col_count = lax.axis_size("col")
    vox_count = lax.axis_size("vox")
    subjects = sub_rows * row_count * col_count
    half_groups = row_count // vox_count
    vox_pos = lax.axis_index("vox")
    flat = maps.astype(jnp.float32)
    totals = lax.psum(jnp.sum(flat, axis=0), ("row", "col"))
    centered = (flat - totals[None, :] / subjects).astype(jnp.bfloat16)
    own_start = vox_pos * half_groups * sub_rows
    own_count = half_groups * sub_rows
    partial_sketch = None
    col_maps, col_probes = (
        lax.all_gather(centered, "row", axis=0, tiled=True),
        lax.all_gather(probes, "row", axis=0, tiled=True),
    )
    tile = block_product(lax.all_gather(centered, "col", axis=0, tiled=True), col_maps)
    block_rows = tile.shape[0]
    gram = lax.psum_scatter(
        tile.reshape(block_rows, row_count, 1, sub_rows), "vox", scatter_dimension=1, tiled=True
    )
    own_probes = lax.dynamic_slice_in_dim(col_probes, own_start, own_count, 0)
    partial_sketch = jnp.dot(
        gram.reshape(block_rows, own_count),
        own_probes.astype(jnp.float32),
        precision=lax.Precision.HIGHEST,
    )
    sketch = lax.psum_scatter(partial_sketch, ("col", "vox"), scatter_dimension=0, tiled=True)
    local_cross = lax.dot_general(
        sketch, sketch, (((0,), (0,)), ((), ())), precision=lax.Precision.HIGHEST
    )
    cross = lax.psum(local_cross, ("row", "col", "vox")) / subjects
    lower = jnp.linalg.cholesky(cross)
    basis = jax.scipy.linalg.solve_triangular(lower, sketch.T, lower=True).T
    return (gram, basis, lower.T)


def solution(mesh):
    placed = (P(("row", "col"), "vox"), P(("row", "col"), None))
    return jax.shard_map(
        shards,
        mesh=mesh,
        in_specs=placed,
        out_specs=(P("row", "vox", "col", None), P(("row", "col", "vox"), None), P()),
        check_vma=False,
    )
```

profile of v0, /device:TPU:2, one launch (start us, length us, event | category | flops | bytes accessed | tf_op | source)
XLA Modules:
  0.0 926.2 jit_solution(6317984655225748700)
XLA Ops:
  7.2 0.0 all-gather.5.cloned.1.call-start
  7.2 1.0 convert_reduce_fusion
  8.2 342.4 %psum.14 = f32[1024]{0:T(1024)S(1)} all-reduce(f32[1024]{0:T(1024)S(1)} %convert_reduce_fusion), channel_id=1, replica_groups=mesh['row'=8,'col'=16,'vox'=2] {'row','col'}, use_global_device_ids=true, to_apply=%region_1.0 | all-reduce | flops 1024 | bytes 8192 | tf_op jit(solution)/shard_map/psum | solution.py:27
  350.6 1.7 fusion
  352.3 0.0 all-gather.5.cloned.1.call-update
  352.3 0.0 all-gather.3.cloned.1.call-start
  352.4 0.7 all-gather.3.cloned.1.call-update
  353.1 0.0 reduce-scatter.3.cloned.1.call-start
  353.1 42.8 %all-gather.5.cloned.1.call-done = bf16[1024,1024]{1,0:T(8,128)(2,1)} async-done(((bf16[128,1024]{1,0:T(8,128)(2,1)}), bf16[1024,1024]{1,0:T(8,128)(2,1)}) %all-gather.5.cloned.1.call-update) | async-done | bytes 2097168 | tf_op jit(solution)/shard_map/all_gather | solution.py:33
  396.0 58.1 %all-gather.3.cloned.1.call-done = bf16[2048,1024]{1,0:T(8,128)(2,1)} async-done(((bf16[128,1024]{1,0:T(8,128)(2,1)}), bf16[2048,1024]{1,0:T(8,128)(2,1)}) %all-gather.3.cloned.1.call-update) | async-done | bytes 4194320 | tf_op jit(solution)/shard_map/all_gather | solution.py:36
  454.1 10.6 %convolution_multiply_fusion = f32[2048,1024]{0,1:T(8,128)} fusion(bf16[2048,1024]{1,0:T(8,128)(2,1)} %all-gather.3.cloned.1.call-done, bf16[1024,1024]{1,0:T(8,128)(2,1)} %all-gather.5.cloned.1.call-done), kind=kOutput, calls=%fused_computation.2 | convolution fusion | flops 4297064448 | bytes 14680064 | tf_op jit(solution)/shard_map/dot_general | solution.py:11
  464.7 9.1 copy.14
  473.8 0.0 copy-start.1
  473.8 0.0 reduce-scatter.3.cloned.1.call-update
  473.9 0.0 reduce-scatter.5.cloned.1.call-start
  473.9 0.8 copy-done.1
  474.7 26.8 %all_gather.11 = bf16[1024,256]{1,0:T(8,128)(2,1)S(1)} all-gather(bf16[128,256]{1,0:T(8,128)(2,1)S(1)} %copy-done.1), channel_id=1, replica_groups=mesh['row'=8,'col'=16,'vox'=2] {'row'}, dimensions={0}, use_global_device_ids=true | all-gather | bytes 589824 | tf_op jit(solution)/shard_map/all_gather | solution.py:34
  501.4 5.3 copy.15
  506.8 7.0 fusion.2
  513.7 0.0 reduce-scatter.5.cloned.1.call-update
  513.8 0.2 all-reduce.3.cloned.1.call-start
  514.0 84.6 %reduce-scatter.5.cloned.1.call-done = f32[64,256]{1,0:T(8,128)} async-done(((f32[2048,256]{1,0:T(8,128)}), f32[64,256]{1,0:T(8,128)}) %reduce-scatter.5.cloned.1.call-update) | async-done | bytes 65552 | tf_op jit(solution)/shard_map/reduce_scatter | solution.py:47
  598.6 2.0 fusion.15
  600.6 0.0 all-reduce.3.cloned.1.call-update
  600.6 8.4 copy.18
  609.1 246.4 %all-reduce.3.cloned.1.call-done = f32[256,256]{0,1:T(8,128)} async-done(((f32[256,256]{0,1:T(8,128)}), f32[256,256]{0,1:T(8,128)}) %all-reduce.3.cloned.1.call-update) | async-done | bytes 262160 | tf_op jit(solution)/shard_map/psum | solution.py:51
  855.5 1.0 broadcast_multiply_fusion
  856.4 0.1 copy.17
  856.6 1.0 fusion.1
  857.6 11.7 %cholesky.50 = f32[128,128]{1,0:T(8,128)S(1)} custom-call(f32[128,128]{1,0:T(8,128)S(1)} %cholesky.118), custom_call_target="Cholesky" | custom-call | tf_op jit(solution)/shard_map/jit(cholesky)/cholesky | solution.py:52
  869.3 9.8 %custom-call.15 = f32[1,128,128]{1,2,0:T(8,128)S(1)} custom-call(f32[1,128,128]{2,1,0:T(8,128)S(1)} %get-tuple-element.35), custom_call_target="InvertDiagBlocksLowerTriangular" | custom-call | tf_op jit(solution)/shard_map/jit(cholesky)/cholesky | solution.py:52
  879.1 0.2 constant_dynamic-update-slice_fusion.1
  879.4 0.3 convolution_subtract_fusion
  879.6 11.7 %cholesky.105 = f32[128,128]{1,0:T(8,128)S(1)} custom-call(f32[128,128]{1,0:T(8,128)S(1)} %convolution_subtract_fusion), custom_call_target="Cholesky" | custom-call | tf_op jit(solution)/shard_map/jit(cholesky)/cholesky | solution.py:52
  891.4 0.7 compare_reduce_fusion
  893.5 0.1 triangular_solve.57
  893.6 4.1 while.1
  893.6 0.6 fusion.26
  894.2 1.4 bitcast_dynamic-update-slice_fusion.2
  895.6 0.6 fusion.26
  896.2 1.4 bitcast_dynamic-update-slice_fusion.2
  897.7 19.9 %custom-call.16 = f32[2,128,128]{1,2,0:T(8,128)S(1)} custom-call(f32[2,128,128]{2,1,0:T(8,128)S(1)} %get-tuple-element.10), custom_call_target="InvertDiagBlocksLowerTriangular" | custom-call | tf_op jit(solution)/shard_map/jit(_solve_triangular)/triangular_solve | solution.py:53
  917.6 0.0 copy-done
  917.6 0.2 fusion.8
  917.8 0.2 convolution_subtract_fusion.1
  918.0 0.2 fusion.7
  918.2 0.6 maximum_bitcast_fusion
  918.8 0.8 copy.19
  (12 shorter events, 0.2 us)
Async XLA Ops:
  7.2 388.8 %all-gather.5.cloned.1.call-start = ((), (), s32[]{:S(2)}) async-start(), calls=%async_computation.3 | async-start | bytes 2359296 | tf_op jit(solution)/shard_map/all_gather | solution.py:33
  352.3 101.7 %all-gather.3.cloned.1.call-start = ((), (), s32[]{:S(2)}) async-start(), calls=%async_computation.2 | async-start | bytes 4456448 | tf_op jit(solution)/shard_map/all_gather | solution.py:36
  353.1 148.3 %reduce-scatter.3.cloned.1.call-start = ((), (), s32[]{:S(2)}) async-start(), calls=%async_computation.4 | async-start | bytes 12582912 | tf_op jit(solution)/shard_map/reduce_scatter | solution.py:38
  473.8 0.8 copy-start.1
  473.9 124.7 %reduce-scatter.5.cloned.1.call-start = ((), (), s32[]{:S(2)}) async-start(), calls=%async_computation.5 | async-start | bytes 2162688 | tf_op jit(solution)/shard_map/reduce_scatter | solution.py:47
  513.8 341.7 %all-reduce.3.cloned.1.call-start = ((), (), s32[]{:S(2)}) async-start(), calls=%async_computation.6 | async-start | bytes 524288 | tf_op jit(solution)/shard_map/psum | solution.py:51
  609.1 308.5 %copy-start = (f32[64,256]{1,0:T(8,128)S(1)}, f32[64,256]{1,0:T(8,128)}, u32[]{:S(2)}) copy-start(f32[64,256]{1,0:T(8,128)} %reduce-scatter.5.cloned.1.call-done) | copy-start | bytes 196612
Sparse Core Ops, SparseCore 0:
  352.5 43.4 all-gather.4
  399.0 55.0 all-gather.2
  474.0 21.9 reduce-scatter.2
  513.9 84.6 reduce-scatter.4
  605.3 250.0 all-reduce.2
where the time goes:
time: 927 us; the launch traced here: 926 us
  waiting for transfers between devices  433 us (47%)
  blocking collectives  369 us (40%)
  other arithmetic  59.3 us (6%)
  local copies, waits for them, and re-layouts  28.8 us (3%)
  matrix products  20.7 us (2%)
  between operations  15.2 us (2%)
    psum x1, blocking collectives, shards(): totals = lax.psum(jnp.sum(flat, axis=0), ('row', 'col'))  342 us
    psum x1, waiting for transfers between devices, shards(): cross = lax.psum(local_cross, ('row', 'col', 'vox')) / subjects  246 us
    reduce_scatter x1, waiting for transfers between devices, shards(): lax.psum_scatter(partial_sketch, ('col', 'vox'), scatter_dimension=0, til...  84.6 us
    all_gather x1, waiting for transfers between devices, shards(): lax.all_gather(centered, 'col', axis=0, tiled=True)  58.1 us
    all_gather x1, waiting for transfers between devices, shards(): lax.all_gather(centered, 'row', axis=0, tiled=True)  42.8 us
    another operation x6, other arithmetic, shards(): lower = jnp.linalg.cholesky(cross)  34 us
    all_gather x1, blocking collectives, shards(): lax.all_gather(probes, 'row', axis=0, tiled=True)  26.8 us
    another operation x2, other arithmetic, shards(): basis = jax.scipy.linalg.solve_triangular(lower, sketch.T, lower=True).T  19.9 us
  transfers between devices with their start and end apart: 5, of which 4 were waited for; matrix products, arithmetic and copies ran while one was open for 1% of the time, Pallas kernels for 0%

commit v1 on v0

--- a/solution.py
+++ b/solution.py
@@ -48,7 +48,7 @@
     local_cross = lax.dot_general(
         sketch, sketch, (((0,), (0,)), ((), ())), precision=lax.Precision.HIGHEST
     )
-    cross = lax.psum(local_cross, ("row", "col", "vox")) / subjects
+    cross = lax.psum(lax.psum(local_cross, ("col", "vox")), "row") / subjects
     lower = jnp.linalg.cholesky(cross)
     basis = jax.scipy.linalg.solve_triangular(lower, sketch.T, lower=True).T
     return (gram, basis, lower.T)

time: 927 us -> 860 us (0.928)
  waiting for transfers between devices: 433 us -> 365 us
    psum x1 -> x2, waiting for transfers between devices: 246 us -> 179 us  [shards(): cross = lax.psum(lax.psum(local_cross, ('col', 'vox')), 'row') / subjects]
  transfers between devices with their start and end apart: 5 -> 6, of which waited for: 4 -> 5; matrix products, arithmetic and copies ran while one was open for 1% -> 1% of each run, Pallas kernels for 0% -> 0%
where the time goes in v1:
time: 860 us; the launch traced here: 859 us
  blocking collectives  369 us (43%)
  waiting for transfers between devices  365 us (42%)
  other arithmetic  59.3 us (7%)
  local copies, waits for them, and re-layouts  28.8 us (3%)
  matrix products  20.7 us (2%)
  between operations  15.6 us (2%)
    psum x1, blocking collectives, shards(): totals = lax.psum(jnp.sum(flat, axis=0), ('row', 'col'))  342 us
    psum x2, waiting for transfers between devices, shards(): cross = lax.psum(lax.psum(local_cross, ('col', 'vox')), 'row') / subjects  179 us
    reduce_scatter x1, waiting for transfers between devices, shards(): lax.psum_scatter(partial_sketch, ('col', 'vox'), scatter_dimension=0, til...  84.7 us
    all_gather x1, waiting for transfers between devices, shards(): lax.all_gather(centered, 'col', axis=0, tiled=True)  58.1 us
    all_gather x1, waiting for transfers between devices, shards(): lax.all_gather(centered, 'row', axis=0, tiled=True)  42.8 us
    another operation x6, other arithmetic, shards(): lower = jnp.linalg.cholesky(cross)  34 us
    all_gather x1, blocking collectives, shards(): lax.all_gather(probes, 'row', axis=0, tiled=True)  26.8 us
    another operation x2, other arithmetic, shards(): basis = jax.scipy.linalg.solve_triangular(lower, sketch.T, lower=True).T  19.9 us
  transfers between devices with their start and end apart: 6, of which 5 were waited for; matrix products, arithmetic and copies ran while one was open for 1% of the time, Pallas kernels for 0%

profile of v1, /device:TPU:2, one launch (start us, length us, event | category | flops | bytes accessed | tf_op | source)
XLA Modules:
  0.0 859.2 jit_solution(5199812671608712795)
XLA Ops:
  7.2 0.0 all-gather.5.cloned.1.call-start
  7.2 1.0 convert_reduce_fusion
  8.2 342.4 %psum.21 = f32[1024]{0:T(1024)S(1)} all-reduce(f32[1024]{0:T(1024)S(1)} %convert_reduce_fusion), channel_id=1, replica_groups=mesh['row'=8,'col'=16,'vox'=2] {'row','col'}, use_global_device_ids=true, to_apply=%region_1.0 | all-reduce | flops 1024 | bytes 8192 | tf_op jit(solution)/shard_map/psum | solution.py:27
  350.6 1.7 fusion
  352.3 0.0 all-gather.5.cloned.1.call-update
  352.3 0.0 all-gather.3.cloned.1.call-start
  352.4 0.7 all-gather.3.cloned.1.call-update
  353.1 0.0 reduce-scatter.3.cloned.1.call-start
  353.1 42.8 %all-gather.5.cloned.1.call-done = bf16[1024,1024]{1,0:T(8,128)(2,1)} async-done(((bf16[128,1024]{1,0:T(8,128)(2,1)}), bf16[1024,1024]{1,0:T(8,128)(2,1)}) %all-gather.5.cloned.1.call-update) | async-done | bytes 2097168 | tf_op jit(solution)/shard_map/all_gather | solution.py:33
  396.0 58.1 %all-gather.3.cloned.1.call-done = bf16[2048,1024]{1,0:T(8,128)(2,1)} async-done(((bf16[128,1024]{1,0:T(8,128)(2,1)}), bf16[2048,1024]{1,0:T(8,128)(2,1)}) %all-gather.3.cloned.1.call-update) | async-done | bytes 4194320 | tf_op jit(solution)/shard_map/all_gather | solution.py:36
  454.1 10.6 %convolution_multiply_fusion = f32[2048,1024]{0,1:T(8,128)} fusion(bf16[2048,1024]{1,0:T(8,128)(2,1)} %all-gather.3.cloned.1.call-done, bf16[1024,1024]{1,0:T(8,128)(2,1)} %all-gather.5.cloned.1.call-done), kind=kOutput, calls=%fused_computation.2 | convolution fusion | flops 4297064448 | bytes 14680064 | tf_op jit(solution)/shard_map/dot_general | solution.py:11
  464.7 9.1 %copy.14 = f32[2048,8,1,128]{3,0,2,1:T(8,128)} copy(f32[2048,8,1,128]{0,3,1,2:T(8,128)} %bitcast.44) | data formatting | bytes 16777216 | tf_op jit(solution)/shard_map/reshape | solution.py:39
  473.8 0.0 reduce-scatter.3.cloned.1.call-update
  473.9 0.0 reduce-scatter.5.cloned.1.call-start
  473.9 0.8 copy-done.1
  474.7 26.8 %all_gather.11 = bf16[1024,256]{1,0:T(8,128)(2,1)S(1)} all-gather(bf16[128,256]{1,0:T(8,128)(2,1)S(1)} %copy-done.1), channel_id=1, replica_groups=mesh['row'=8,'col'=16,'vox'=2] {'row'}, dimensions={0}, use_global_device_ids=true | all-gather | bytes 589824 | tf_op jit(solution)/shard_map/all_gather | solution.py:34
  501.4 5.3 copy.15
  506.8 7.0 fusion.2
  513.8 0.0 all-reduce.4.cloned.1.call-start
  513.8 84.7 %reduce-scatter.5.cloned.1.call-done = f32[64,256]{1,0:T(8,128)} async-done(((f32[2048,256]{1,0:T(8,128)}), f32[64,256]{1,0:T(8,128)}) %reduce-scatter.5.cloned.1.call-update) | async-done | bytes 65552 | tf_op jit(solution)/shard_map/reduce_scatter | solution.py:47
  598.6 2.0 fusion.15
  600.6 0.0 all-reduce.4.cloned.1.call-update
  600.6 0.2 all-reduce.6.cloned.1.call-start
  600.8 112.3 %all-reduce.4.cloned.1.call-done = f32[256,256]{0,1:T(8,128)} async-done(((f32[256,256]{0,1:T(8,128)}), f32[256,256]{0,1:T(8,128)}) %all-reduce.4.cloned.1.call-update) | async-done | bytes 262160 | tf_op jit(solution)/shard_map/psum | solution.py:51
  713.2 0.0 all-reduce.6.cloned.1.call-update
  713.2 8.4 copy.18
  721.7 66.4 %all-reduce.6.cloned.1.call-done = f32[256,256]{0,1:T(8,128)} async-done(((f32[256,256]{0,1:T(8,128)}), f32[256,256]{0,1:T(8,128)}) %all-reduce.6.cloned.1.call-update) | async-done | bytes 262160 | tf_op jit(solution)/shard_map/psum | solution.py:51
  788.1 1.0 broadcast_multiply_fusion
  789.1 0.1 copy.17
  789.2 1.0 fusion.1
  790.2 11.7 %cholesky.50 = f32[128,128]{1,0:T(8,128)S(1)} custom-call(f32[128,128]{1,0:T(8,128)S(1)} %cholesky.118), custom_call_target="Cholesky" | custom-call | tf_op jit(solution)/shard_map/jit(cholesky)/cholesky | solution.py:52
  802.0 9.8 %custom-call.15 = f32[1,128,128]{1,2,0:T(8,128)S(1)} custom-call(f32[1,128,128]{2,1,0:T(8,128)S(1)} %get-tuple-element.35), custom_call_target="InvertDiagBlocksLowerTriangular" | custom-call | tf_op jit(solution)/shard_map/jit(cholesky)/cholesky | solution.py:52
  811.8 0.2 constant_dynamic-update-slice_fusion.1
  812.0 0.3 convolution_subtract_fusion
  812.3 11.7 %cholesky.105 = f32[128,128]{1,0:T(8,128)S(1)} custom-call(f32[128,128]{1,0:T(8,128)S(1)} %convolution_subtract_fusion), custom_call_target="Cholesky" | custom-call | tf_op jit(solution)/shard_map/jit(cholesky)/cholesky | solution.py:52
  824.0 0.7 compare_reduce_fusion
  826.2 0.1 triangular_solve.57
  826.2 4.1 while.1
  826.2 0.6 fusion.26
  826.8 1.4 bitcast_dynamic-update-slice_fusion.2
  828.3 0.6 fusion.26
  828.9 1.4 bitcast_dynamic-update-slice_fusion.2
  830.3 19.9 %custom-call.16 = f32[2,128,128]{1,2,0:T(8,128)S(1)} custom-call(f32[2,128,128]{2,1,0:T(8,128)S(1)} %get-tuple-element.10), custom_call_target="InvertDiagBlocksLowerTriangular" | custom-call | tf_op jit(solution)/shard_map/jit(_solve_triangular)/triangular_solve | solution.py:53
  850.2 0.2 fusion.8
  850.4 0.2 convolution_subtract_fusion.1
  850.7 0.2 fusion.7
  850.9 0.6 maximum_bitcast_fusion
  851.5 0.8 copy.19
  (15 shorter events, 0.2 us)
Async XLA Ops:
  7.2 388.8 %all-gather.5.cloned.1.call-start = ((), (), s32[]{:S(2)}) async-start(), calls=%async_computation.3 | async-start | bytes 2359296 | tf_op jit(solution)/shard_map/all_gather | solution.py:33
  352.3 101.7 %all-gather.3.cloned.1.call-start = ((), (), s32[]{:S(2)}) async-start(), calls=%async_computation.2 | async-start | bytes 4456448 | tf_op jit(solution)/shard_map/all_gather | solution.py:36
  353.1 148.3 %reduce-scatter.3.cloned.1.call-start = ((), (), s32[]{:S(2)}) async-start(), calls=%async_computation.4 | async-start | bytes 12582912 | tf_op jit(solution)/shard_map/reduce_scatter | solution.py:38
  473.8 0.8 copy-start.1
  473.9 124.7 %reduce-scatter.5.cloned.1.call-start = ((), (), s32[]{:S(2)}) async-start(), calls=%async_computation.5 | async-start | bytes 2162688 | tf_op jit(solution)/shard_map/reduce_scatter | solution.py:47
  513.8 199.4 %all-reduce.4.cloned.1.call-start = ((), (), s32[]{:S(2)}) async-start(), calls=%async_computation.6 | async-start | bytes 524288 | tf_op jit(solution)/shard_map/psum | solution.py:51
  600.6 187.5 %all-reduce.6.cloned.1.call-start = ((), (), s32[]{:S(2)}) async-start(), calls=%async_computation.7 | async-start | bytes 524288 | tf_op jit(solution)/shard_map/psum | solution.py:51
  721.7 128.6 %copy-start = (f32[64,256]{1,0:T(8,128)S(1)}, f32[64,256]{1,0:T(8,128)}, u32[]{:S(2)}) copy-start(f32[64,256]{1,0:T(8,128)} %reduce-scatter.5.cloned.1.call-done) | copy-start | bytes 196612
Sparse Core Ops, SparseCore 0:
  352.5 43.4 all-gather.4
  399.0 55.0 all-gather.2
  474.0 21.9 reduce-scatter.2
  513.9 84.6 reduce-scatter.4
  602.5 110.6 all-reduce.3
  715.4 72.7 all-reduce.5
